TPU v7x, 32 devices: a whole 2x2x4 slice. The times are simulated.
32 devices in a mesh: grp: 2 (over x), tile: 16 (over z, y, core).
Axes of the slice: x: 2, y: 2, z: 4, core: 2. Of those that a mesh axis runs over, the one named last changes fastest.
Arguments:
- full_resolution_frames: bfloat16 [32, 2, 512, 512], P(('grp', 'tile')), parts along dimension 0, may hold values from -24 to 24
- height_angle_factor: float32 [1024, 512], P('grp'), parts along dimension 0, may hold values from -4 to 4
- normal_spacings: float32 [32], P('grp'), parts along dimension 0, may hold values from -2 to 2
- couple_entry_flags: int32 [16, 3], replicated, may hold values from 0 to 1, as said below
- block_target_indices: int32 [32, 64], P('grp'), parts along dimension 0, may hold values from 0 to 255, as said below
- block_target_totals: int32 [32], P('grp'), parts along dimension 0, may hold values from 1 to 64, as said below
Outputs:
- coherence: float32 [32, 3, 128, 32], P(('grp', 'tile')), parts along dimension 0
- velocities: float32 [2048, 15], P(('grp', 'tile')), parts along dimension 0
There are 2 independent parts, one for each index of `grp`. A program takes and returns all parts, laid end to end along the dimension named above; an argument that names none is the same for every part. Nothing has to cross between parts.
Inputs may be any that keep to these rules, and one draw needn't show every extreme that they name: `couple_entry_flags`: slot k-1 of date d stands for the pair of d and d + k; slot 0 is 1 wherever d + 1 < 16; slots with d + k >= 16 are 0. `block_target_indices`: row t lists distinct looked pixels of tile t; entries at or past the tile's count are 0. `block_target_totals`: some tile has exactly 64.
All inputs are finite; a program needn't handle non-finite values.
Results may differ from a plain program's by a relative error of at most 0.0003.
Values may be sent and summed in bfloat16 or wider, within the bound.
A program may use at most 192 MiB of HBM per device.

v0:
```python
import jax
import jax.numpy as jnp
from jax import lax
from jax.sharding import PartitionSpec as P

LOOK_ROWS = 4
LOOK_COLS = 16
EPSILON = 1e-06


def from_behind(block, axis, distance):
    devices = range(lax.axis_size(axis))
    route = [(i - distance, i) for i in devices if i - distance in devices]
    return lax.ppermute(block, axis, route)


def pooling_matrix(cols):
    column_index = jnp.arange(cols, dtype=jnp.int32)[:, None]
    look_index = jnp.arange(cols // LOOK_COLS, dtype=jnp.int32)[None, :]
    member = (column_index // LOOK_COLS == look_index).astype(jnp.float32)
    return member * (1.0 / (LOOK_ROWS * LOOK_COLS))


def looked(field, pooling):
    rows = field.shape[-2]
    cols = field.shape[-1]
    row_sums = jnp.sum(
        field.reshape(field.shape[:-2] + (rows // LOOK_ROWS, LOOK_ROWS, cols)), axis=-2
    )
    return jnp.einsum("...c,cl->...l", row_sums, pooling, precision=lax.Precision.HIGHEST)


def own_power(own_real, own_imag, pooling):
    return looked(own_real * own_real + own_imag * own_imag, pooling)


def pair_stats(own_real, own_imag, power_own, other_real, other_imag, theta, pooling):
    cross_real = own_real * other_real + own_imag * other_imag
    cross_imag = own_imag * other_real - own_real * other_imag
    cosine = jnp.cos(theta)
    sine = jnp.sin(theta)
    flat_real = cross_real * cosine + cross_imag * sine
    flat_imag = cross_imag * cosine - cross_real * sine
    other_energy = other_real * other_real + other_imag * other_imag
    means = looked(jnp.stack([flat_real, flat_imag, other_energy], axis=0), pooling)
    mean_real = means[0]
    mean_imag = means[1]
    power_other = means[2]
    scale = 1.0 / jnp.sqrt(power_own * power_other + EPSILON)
    return (jnp.sqrt(mean_real * mean_real + mean_imag * mean_imag) * scale, mean_imag * scale)


def inverse_map(couple_entry_flags):
    dates = couple_entry_flags.shape[0]
    later_mates = couple_entry_flags.shape[1]
    count = dates * later_mates
    pair_index = jnp.arange(count, dtype=jnp.int32)
    first_date = pair_index // later_mates
    pair_span = pair_index % later_mates + 1
    interval_index = jnp.arange(dates - 1, dtype=jnp.int32)
    covered = (interval_index[None, :] >= first_date[:, None]) & (
        interval_index[None, :] < (first_date + pair_span)[:, None]
    )
    design = couple_entry_flags.reshape(count).astype(jnp.float32)[:, None] * covered.astype(
        jnp.float32
    )
    normal = jnp.dot(design.T, design, precision=lax.Precision.HIGHEST)
    factor = jnp.linalg.cholesky(normal)
    partial_solve = lax.linalg.triangular_solve(factor, design.T, left_side=True, lower=True)
    return lax.linalg.triangular_solve(
        factor, partial_solve, left_side=True, lower=True, transpose_a=True
    )


def local(
    full_resolution_frames,
    height_angle_factor,
    normal_spacings,
    couple_entry_flags,
    block_target_indices,
    block_target_totals,
):
    tile_count = lax.axis_size("tile")
    entry_location = lax.axis_index("tile")
    dates = couple_entry_flags.shape[0]
    later_mates = couple_entry_flags.shape[1]
    image_rows = height_angle_factor.shape[0]
    image_cols = height_angle_factor.shape[1]
    tile_rows = image_rows // tile_count
    looked_cols = image_cols // LOOK_COLS
    tile_pix = tile_rows // LOOK_ROWS * looked_cols
    slot_count = block_target_indices.shape[1]
    pooling = pooling_matrix(image_cols)
    slots = lax.dynamic_index_in_dim(block_target_indices, entry_location, 0, keepdims=False)
    spacing_extended = jnp.concatenate(
        [normal_spacings, jnp.zeros((later_mates,), normal_spacings.dtype)], axis=0
    )
    own = full_resolution_frames[0].astype(jnp.float32)
    power_own = own_power(own[0], own[1], pooling)
    reference_spacing = lax.dynamic_index_in_dim(normal_spacings, entry_location, 0, keepdims=False)
    cohs = []
    phases = []
    for offset in range(1, later_mates + 1):
        other = from_behind(full_resolution_frames, "tile", -offset)[0].astype(jnp.float32)
        other_base = lax.dynamic_index_in_dim(
            spacing_extended, entry_location + offset, 0, keepdims=False
        )
        theta = (reference_spacing - other_base) * height_angle_factor
        coh, phase = pair_stats(own[0], own[1], power_own, other[0], other[1], theta, pooling)
        cohs.append(coh)
        phases.append(phase)
    coh_stack = jnp.stack(cohs, axis=0)
    phase_stack = jnp.stack(phases, axis=0)
    mask_row = lax.dynamic_slice_in_dim(couple_entry_flags, entry_location, 1, 0).astype(
        jnp.float32
    )
    coherence = coh_stack[None] * mask_row[:, :, None, None]
    phase_local = phase_stack[None]
    arrived = lax.all_to_all(phase_local, "tile", split_axis=2, concat_axis=0, tiled=True)
    phase_tile = arrived.reshape(dates * later_mates, tile_pix)
    picked = jnp.take(phase_tile, slots, axis=1)
    mapping = inverse_map(couple_entry_flags)
    velocities = jnp.dot(picked.T, mapping.T, precision=lax.Precision.HIGHEST)
    own_count = lax.dynamic_index_in_dim(block_target_totals, entry_location, 0, keepdims=False)
    valid = (jnp.arange(slot_count, dtype=jnp.int32) < own_count).astype(jnp.float32)
    return (coherence, velocities * valid[:, None])


def solution(mesh):
    in_specs = (
        P(("grp", "tile"), None, None, None),
        P("grp", None),
        P("grp"),
        P(),
        P("grp", None),
        P("grp"),
    )
    out_specs = (P(("grp", "tile"), None, None, None), P(("grp", "tile"), None))
    return jax.shard_map(local, mesh=mesh, in_specs=in_specs, out_specs=out_specs, check_vma=False)
```

profile of v0, /device:TPU:0, one launch (start us, length us, event | category | flops | bytes accessed | tf_op | source)
XLA Modules:
  0.0 135.5 jit_solution(10515715587612405986)
XLA Ops:
  0.6 1.4 %collective-permute-start = (bf16[1,2,512,512]{3,2,1,0:T(8,128)(2,1)}, bf16[1,2,512,512]{3,2,1,0:T(8,128)(2,1)}, u32[]{:S(2)}, u32[]{:S(2)}) collective-permute-start(bf16[1,2,512,512]{3,2,1,0:T(8,128)(2,1)} %param.6), channel_id=1, source_target_pairs={{1,0},{2,1},{3,2},{4,3},{5,4},{6,5},{7,6},{8,7},{9,8},{10,9},{11,1... | collective-permute-start | bytes 3145736 | tf_op jit(solution)/shard_map/ppermute | solution.py:14
  2.1 1.3 collective-permute-start.2
  3.4 1.3 collective-permute-start.1
  4.7 1.5 %convert_element_type.38 = f32[1,2,512,512]{3,2,1,0:T(8,128)S(1)} convert(bf16[1,2,512,512]{3,2,1,0:T(8,128)(2,1)} %param.6) | non-fusion elementwise | flops 524288 | bytes 3145728 | tf_op jit(solution)/shard_map/convert_element_type | solution.py:98
  6.8 1.4 %cholesky.16 = f32[15,15]{1,0:T(8,128)S(1)} custom-call(f32[15,15]{1,0:T(8,128)S(1)} %fusion.69), custom_call_target="Cholesky" | custom-call | tf_op jit(solution)/shard_map/jit(cholesky)/cholesky | solution.py:68
  11.1 1.3 compare_convert_fusion
  17.0 1.3 add.193
  19.4 1.9 %reduce_sum.37 = f32[128,512]{1,0:T(8,128)S(1)} reduce(f32[128,4,512]{2,1,0:T(4,128)} %add.193, f32[]{:T(128)} %constant.122.clone.1), dimensions={1}, to_apply=%region_1.2 | reduce | flops 196608 | bytes 1310724 | tf_op jit(solution)/shard_map/reduce_sum | solution.py:27
  21.7 1.5 %convert_element_type.39 = f32[1,2,512,512]{3,2,1,0:T(8,128)S(1)} convert(bf16[1,2,512,512]{3,2,1,0:T(8,128)(2,1)} %collective-permute-done) | non-fusion elementwise | flops 524288 | bytes 3145728 | tf_op jit(solution)/shard_map/convert_element_type | solution.py:104
  23.2 1.3 copy-done
  24.8 1.3 stack.62
  26.1 5.7 %collective-permute-done.2 = bf16[1,2,512,512]{3,2,1,0:T(8,128)(2,1)} collective-permute-done((bf16[1,2,512,512]{3,2,1,0:T(8,128)(2,1)}, bf16[1,2,512,512]{3,2,1,0:T(8,128)(2,1)}, u32[]{:S(2)}, u32[]{:S(2)}) %collective-permute-start.2) | collective-permute-done | bytes 1048608 | tf_op jit(solution)/shard_map/ppermute | solution.py:14
  31.8 1.5 %convert_element_type.41 = f32[1,2,512,512]{3,2,1,0:T(8,128)S(1)} convert(bf16[1,2,512,512]{3,2,1,0:T(8,128)(2,1)} %collective-permute-done.2) | non-fusion elementwise | flops 524288 | bytes 3145728 | tf_op jit(solution)/shard_map/convert_element_type | solution.py:104
  33.3 1.2 multiply_add_fusion
  34.5 16.1 %collective-permute-done.1 = bf16[1,2,512,512]{3,2,1,0:T(8,128)(2,1)} collective-permute-done((bf16[1,2,512,512]{3,2,1,0:T(8,128)(2,1)}, bf16[1,2,512,512]{3,2,1,0:T(8,128)(2,1)}, u32[]{:S(2)}, u32[]{:S(2)}) %collective-permute-start.1) | collective-permute-done | bytes 1048608 | tf_op jit(solution)/shard_map/ppermute | solution.py:14
  50.6 1.5 %convert_element_type.40 = f32[1,2,512,512]{3,2,1,0:T(8,128)S(1)} convert(bf16[1,2,512,512]{3,2,1,0:T(8,128)(2,1)} %collective-permute-done.1) | non-fusion elementwise | flops 524288 | bytes 3145728 | tf_op jit(solution)/shard_map/convert_element_type | solution.py:104
  52.4 1.3 copy-done.1
  54.0 13.0 %fusion.4 = (f32[512,512]{1,0:T(8,128)}, f32[1,1,512,512]{3,2,1,0:T(8,128)S(1)}, f32[1,1,512,512]{3,2,1,0:T(8,128)S(1)}, f32[512,512]{1,0:T(8,128)}, f32[1,1,512...) fusion(f32[512,512]{1,0:T(8,128)S(1)} %copy-done.10, ...), kind=kLoop, calls=%fused_computation.19 | loop fusion | flops 7864320 | bytes 18874380 | tf_op jit(solution)/shard_map/add | solution.py:42
  67.0 12.5 %fusion.5 = (f32[512,512]{1,0:T(8,128)}, f32[512,512]{1,0:T(8,128)}, f32[512,512]{1,0:T(8,128)}) fusion(f32[1,1,512,512]{3,2,1,0:T(8,128)S(1)} %get-tuple-element.4, f32[1,1,512,512]{3,2,1,0:T(8,128)S(1)} %get-tuple-element.3, f32[512,512]{1,0:T(8,128)S(1)} %copy-done.10, f32[]{:T(128)} %bitcast.1, f32[1,1,512,512]{3,2,1,0:T(8,128)S(1)} %get-tuple-element.16, ...), kind=kLoop, calls=%fused_computation.20 | loop fusion | flops 3145728 | bytes 10485772 | tf_op jit(solution)/shard_map/sub | solution.py:43
  79.5 2.7 %stack.61 = f32[1,128,4,512]{3,2,1,0:T(4,128)} reshape(f32[512,512]{1,0:T(8,128)} %get-tuple-element.17) | data formatting | bytes 2097152 | tf_op jit(solution)/shard_map/stack | solution.py:45
  82.2 1.3 stack.60
  83.5 1.3 stack.72
  84.8 2.7 %stack.71 = f32[1,128,4,512]{3,2,1,0:T(4,128)} reshape(f32[512,512]{1,0:T(8,128)} %get-tuple-element.19) | data formatting | bytes 2097152 | tf_op jit(solution)/shard_map/stack | solution.py:45
  87.5 1.3 stack.70
  88.8 3.9 %maximum_reduce_fusion = f32[3,128,512]{2,1,0:T(8,128)S(1)} fusion(f32[1,128,4,512]{3,2,1,0:T(4,128)S(1)} %copy-done.6, f32[1,128,4,512]{3,2,1,0:T(4,128)} %stack.61, f32[1,128,4,512]{3,2,1,0:T(4,128)} %stack.60), kind=kLoop, calls=%fused_computation.1 | loop fusion | flops 2162688 | bytes 3932160 | tf_op jit(solution)/shard_map/reduce_sum | solution.py:27
  93.6 2.2 %maximum_reduce_fusion.2 = f32[3,128,512]{2,1,0:T(8,128)S(1)} fusion(f32[1,128,4,512]{3,2,1,0:T(4,128)S(1)} %copy-done.7, f32[1,128,4,512]{3,2,1,0:T(4,128)S(1)} %copy-done.8, f32[1,128,4,512]{3,2,1,0:T(4,128)S(1)} %copy-done.9), kind=kLoop, calls=%fused_computation.3 | loop fusion | flops 2162688 | bytes 3932160 | tf_op jit(solution)/shard_map/reduce_sum | solution.py:27
  96.9 1.5 %stack.66 = f32[1,128,4,512]{3,2,1,0:T(4,128)S(1)} reshape(f32[512,512]{1,0:T(8,128)} %get-tuple-element.18) | data formatting | bytes 2097152 | tf_op jit(solution)/shard_map/stack | solution.py:45
  98.5 1.3 stack.65
  99.8 3.4 %maximum_reduce_fusion.1 = f32[3,128,512]{2,1,0:T(8,128)S(1)} fusion(f32[1,128,4,512]{3,2,1,0:T(4,128)S(1)} %stack.67, f32[1,128,4,512]{3,2,1,0:T(4,128)S(1)} %stack.66, f32[1,128,4,512]{3,2,1,0:T(4,128)} %stack.65), kind=kLoop, calls=%fused_computation.2 | loop fusion | flops 2162688 | bytes 3932160 | tf_op jit(solution)/shard_map/reduce_sum | solution.py:27
  105.0 1.2 reduce.8
  107.1 18.8 %all-to-all-start = ((f32[16,1,768]{2,1,0:T(1,128)}), f32[16,1,768]{2,1,0:T(1,128)S(1)}, u32[]{:S(2)}, u32[]{:S(2)}) async-start(f32[16,1,768]{2,1,0:T(1,128)} %reshape.283), calls=%async_computation | async-start | bytes 98304 | tf_op jit(solution)/shard_map/all_to_all | solution.py:119
  126.6 6.1 %all-to-all-done = f32[16,1,768]{2,1,0:T(1,128)S(1)} async-done(((f32[16,1,768]{2,1,0:T(1,128)}), f32[16,1,768]{2,1,0:T(1,128)S(1)}, u32[]{:S(2)}, u32[]{:S(2)}) %all-to-all-start) | async-done | bytes 49184 | tf_op jit(solution)/shard_map/all_to_all | solution.py:119
  (67 shorter events, 14.7 us)
Async XLA Ops:
  0.6 5.6 %copy-start.11 = (s32[16,3]{0,1:T(4,128)S(1)}, s32[16,3]{0,1:T(4,128)}, u32[]{:S(2)}) copy-start(s32[16,3]{0,1:T(4,128)} %param.9) | copy-start | bytes 580
  0.6 8.9 %copy-start.13 = (s32[16]{0:T(128)S(1)}, s32[16]{0:T(128)}, u32[]{:S(2)}) copy-start(s32[16]{0:T(128)} %param.11) | copy-start | bytes 196
  0.6 21.0 %collective-permute-start = (bf16[1,2,512,512]{3,2,1,0:T(8,128)(2,1)}, bf16[1,2,512,512]{3,2,1,0:T(8,128)(2,1)}, u32[]{:S(2)}, u32[]{:S(2)}) collective-permute-start(bf16[1,2,512,512]{3,2,1,0:T(8,128)(2,1)} %param.6), channel_id=1, source_target_pairs={{1,0},{2,1},{3,2},{4,3},{5,4},{6,5},{7,6},{8,7},{9,8},{10,9},{11,1... | collective-permute-start | bytes 3145736 | tf_op jit(solution)/shard_map/ppermute | solution.py:14
  2.1 29.7 %collective-permute-start.2 = (bf16[1,2,512,512]{3,2,1,0:T(8,128)(2,1)}, bf16[1,2,512,512]{3,2,1,0:T(8,128)(2,1)}, u32[]{:S(2)}, u32[]{:S(2)}) collective-permute-start(bf16[1,2,512,512]{3,2,1,0:T(8,128)(2,1)} %param.6), channel_id=1, source_target_pairs={{3,0},{4,1},{5,2},{6,3},{7,4},{8,5},{9,6},{10,7},{11,8},{12,9},{13... | collective-permute-start | bytes 3145736 | tf_op jit(solution)/shard_map/ppermute | solution.py:14
  3.4 47.3 %collective-permute-start.1 = (bf16[1,2,512,512]{3,2,1,0:T(8,128)(2,1)}, bf16[1,2,512,512]{3,2,1,0:T(8,128)(2,1)}, u32[]{:S(2)}, u32[]{:S(2)}) collective-permute-start(bf16[1,2,512,512]{3,2,1,0:T(8,128)(2,1)} %param.6), channel_id=1, source_target_pairs={{2,0},{3,1},{4,2},{5,3},{6,4},{7,5},{8,6},{9,7},{10,8},{11,9},{12,... | collective-permute-start | bytes 3145736 | tf_op jit(solution)/shard_map/ppermute | solution.py:14
  6.2 6.4 %copy-start.12 = (f32[16]{0:T(128)S(1)}, f32[16]{0:T(128)}, u32[]{:S(2)}) copy-start(f32[16]{0:T(128)} %param.8) | copy-start | bytes 196
  23.2 1.4 %copy-start = (f32[1,2,512,512]{3,2,1,0:T(8,128)}, f32[1,2,512,512]{3,2,1,0:T(8,128)S(1)}, u32[]{:S(2)}) copy-start(f32[1,2,512,512]{3,2,1,0:T(8,128)S(1)} %convert_element_type.39) | copy-start | bytes 6291460
  52.2 1.6 %copy-start.1 = (f32[1,2,512,512]{3,2,1,0:T(8,128)S(1)}, f32[1,2,512,512]{3,2,1,0:T(8,128)}, u32[]{:S(2)}) copy-start(f32[1,2,512,512]{3,2,1,0:T(8,128)} %copy-done) | copy-start | bytes 6291460
  52.2 1.9 %copy-start.10 = (f32[512,512]{1,0:T(8,128)S(1)}, f32[512,512]{1,0:T(8,128)}, u32[]{:S(2)}) copy-start(f32[512,512]{1,0:T(8,128)} %param.7) | copy-start | bytes 3145732
  79.5 2.7 %copy-start.5 = (f32[512,512]{1,0:T(8,128)S(1)}, f32[512,512]{1,0:T(8,128)}, u32[]{:S(2)}) copy-start(f32[512,512]{1,0:T(8,128)} %get-tuple-element.2) | copy-start | bytes 3145732
  79.5 4.0 %copy-start.3 = (f32[1,1,512,512]{3,2,1,0:T(8,128)S(1)}, f32[1,1,512,512]{3,2,1,0:T(8,128)}, u32[]{:S(2)}) copy-start(f32[1,1,512,512]{3,2,1,0:T(8,128)} %multiply_add_fusion) | copy-start | bytes 3145732
  83.5 4.0 %copy-start.4 = (f32[512,512]{1,0:T(8,128)S(1)}, f32[512,512]{1,0:T(8,128)}, u32[]{:S(2)}) copy-start(f32[512,512]{1,0:T(8,128)} %get-tuple-element.11) | copy-start | bytes 3145732
  84.8 4.0 %copy-start.6 = (f32[1,128,4,512]{3,2,1,0:T(4,128)S(1)}, f32[1,128,4,512]{3,2,1,0:T(4,128)}, u32[]{:S(2)}) copy-start(f32[1,128,4,512]{3,2,1,0:T(4,128)} %stack.62) | copy-start | bytes 3145732
  88.8 4.8 %copy-start.7 = (f32[1,128,4,512]{3,2,1,0:T(4,128)S(1)}, f32[1,128,4,512]{3,2,1,0:T(4,128)}, u32[]{:S(2)}) copy-start(f32[1,128,4,512]{3,2,1,0:T(4,128)} %stack.72) | copy-start | bytes 3145732
  88.8 4.8 %copy-start.8 = (f32[1,128,4,512]{3,2,1,0:T(4,128)S(1)}, f32[1,128,4,512]{3,2,1,0:T(4,128)}, u32[]{:S(2)}) copy-start(f32[1,128,4,512]{3,2,1,0:T(4,128)} %stack.71) | copy-start | bytes 3145732
  88.8 4.8 %copy-start.9 = (f32[1,128,4,512]{3,2,1,0:T(4,128)S(1)}, f32[1,128,4,512]{3,2,1,0:T(4,128)}, u32[]{:S(2)}) copy-start(f32[1,128,4,512]{3,2,1,0:T(4,128)} %stack.70) | copy-start | bytes 3145732
  96.6 1.9 %copy-start.2 = (f32[512,512]{1,0:T(8,128)S(1)}, f32[512,512]{1,0:T(8,128)}, u32[]{:S(2)}) copy-start(f32[512,512]{1,0:T(8,128)} %get-tuple-element.14) | copy-start | bytes 3145732
  107.1 25.6 %all-to-all-start = ((f32[16,1,768]{2,1,0:T(1,128)}), f32[16,1,768]{2,1,0:T(1,128)S(1)}, u32[]{:S(2)}, u32[]{:S(2)}) async-start(f32[16,1,768]{2,1,0:T(1,128)} %reshape.283), calls=%async_computation | async-start | bytes 98304 | tf_op jit(solution)/shard_map/all_to_all | solution.py:119
where the time goes:
time: 136 us; the launch traced here: 135 us
  other arithmetic  53.6 us (39%)
  waiting for transfers between devices  27.9 us (21%)
  starting transfers between devices  22.8 us (17%)
  local copies, waits for them, and re-layouts  22.2 us (16%)
  between operations  4.68 us (3%)
  matrix products  4.33 us (3%)
    ppermute x3, waiting for transfers between devices, from_behind(): return lax.ppermute(block, axis, route)  21.8 us
    all_to_all x1, starting transfers between devices, local(): lax.all_to_all(phase_local, 'tile', split_axis=2, concat_axis=0, tiled=True)  18.8 us
    another operation x9, local copies, waits for them, and re-layouts, pair_stats(): jnp.stack([flat_real, flat_imag, other_energy], axis=0)  13.6 us
    add x1, other arithmetic, pair_stats(): flat_real = cross_real * cosine + cross_imag * sine  13 us
    sub x1, other arithmetic, pair_stats(): flat_imag = cross_imag * cosine - cross_real * sine  12.5 us
    reduce_sum x4, other arithmetic, looked(): jnp.sum(field.reshape(field.shape[:-2] + (rows // LOOK_ROWS, LOOK_ROWS, c...  11.4 us
    all_to_all x1, waiting for transfers between devices, local(): lax.all_to_all(phase_local, 'tile', split_axis=2, concat_axis=0, tiled=True)  6.07 us
    unnamed x31, local copies, waits for them, and re-layouts  4.66 us
  transfers between devices with their start and end apart: 4, of which 3 were waited for; matrix products, arithmetic and copies ran while one was open for 15% of the time, Pallas kernels for 0%

commit v1 on v0

--- a/solution.py
+++ b/solution.py
@@ -116,7 +116,24 @@
     )
     coherence = coh_stack[None] * mask_row[:, :, None, None]
     phase_local = phase_stack[None]
-    arrived = lax.all_to_all(phase_local, "tile", split_axis=2, concat_axis=0, tiled=True)
+    extra = lax.axis_index("tile")
+    local_next = lax.axis_size("tile")
+    q_next, r_now = (local_next, extra)
+    val2 = phase_local.shape[2] // q_next
+    local_out = list(phase_local.shape)
+    local_out[2] = val2
+    u_next = local_out[0]
+    local_out[0] = u_next * q_next
+    arrived = jnp.zeros(local_out, phase_local.dtype)
+    no = 0
+    while no < q_next:
+        block_now = lax.dynamic_slice_in_dim(phase_local, (r_now ^ no) * val2, val2, axis=2)
+        if no:
+            block_now = lax.ppermute(
+                block_now, "tile", [(dev_i, dev_i ^ no) for dev_i in range(q_next)]
+            )
+        arrived = lax.dynamic_update_slice_in_dim(arrived, block_now, (r_now ^ no) * u_next, axis=0)
+        no += 1
     phase_tile = arrived.reshape(dates * later_mates, tile_pix)
     picked = jnp.take(phase_tile, slots, axis=1)
     mapping = inverse_map(couple_entry_flags)

time: 136 us -> 148 us (1.088)
  starting transfers between devices: 22.8 us -> 38.4 us
  other arithmetic: 53.6 us -> 51.5 us
  waiting for transfers between devices: 27.9 us -> 26.1 us
    ppermute x0 -> x15, starting transfers between devices: none -> 34.4 us  [local(): lax.ppermute(block_now, 'tile', [(dev_i, dev_i ^ no) for dev_i in range(q...]
    all_to_all x1 -> x0, starting transfers between devices: 18.8 us -> none  [local(): lax.all_to_all(phase_local, 'tile', split_axis=2, concat_axis=0, tiled=True)]
    all_to_all x1 -> x0, waiting for transfers between devices: 6.07 us -> none  [local(): lax.all_to_all(phase_local, 'tile', split_axis=2, concat_axis=0, tiled=True)]
    ppermute x0 -> x15, waiting for transfers between devices: none -> 4.59 us  [local(): lax.ppermute(block_now, 'tile', [(dev_i, dev_i ^ no) for dev_i in range(q...]
    unnamed x31 -> x28, local copies, waits for them, and re-layouts: 4.66 us -> 2.99 us
    another operation x0 -> x17, local copies, waits for them, and re-layouts: none -> 1.49 us
  transfers between devices with their start and end apart: 4 -> 18, of which waited for: 3 -> 4; matrix products, arithmetic and copies ran while one was open for 15% -> 14% of each run, Pallas kernels for 0% -> 0%
where the time goes in v1:
time: 148 us; the launch traced here: 147 us
  other arithmetic  51.5 us (35%)
  starting transfers between devices  38.4 us (26%)
  waiting for transfers between devices  26.1 us (18%)
  local copies, waits for them, and re-layouts  21.8 us (15%)
  between operations  5.17 us (3%)
  matrix products  4.33 us (3%)
    ppermute x15, starting transfers between devices, local(): lax.ppermute(block_now, 'tile', [(dev_i, dev_i ^ no) for dev_i in range(q...  34.4 us
    ppermute x3, waiting for transfers between devices, from_behind(): return lax.ppermute(block, axis, route)  21.5 us
    another operation x9, local copies, waits for them, and re-layouts, pair_stats(): jnp.stack([flat_real, flat_imag, other_energy], axis=0)  13.7 us
    add x1, other arithmetic, pair_stats(): flat_real = cross_real * cosine + cross_imag * sine  13 us
    sub x1, other arithmetic, pair_stats(): flat_imag = cross_imag * cosine - cross_real * sine  12.5 us
    reduce_sum x4, other arithmetic, looked(): jnp.sum(field.reshape(field.shape[:-2] + (rows // LOOK_ROWS, LOOK_ROWS, c...  11.3 us
    ppermute x15, waiting for transfers between devices, local(): lax.ppermute(block_now, 'tile', [(dev_i, dev_i ^ no) for dev_i in range(q...  4.59 us
    convert_element_type x3, other arithmetic, local(): from_behind(full_resolution_frames, 'tile', -offset)[0].astype(jnp.float32)  4.53 us
  transfers between devices with their start and end apart: 18, of which 4 were waited for; matrix products, arithmetic and copies ran while one was open for 14% of the time, Pallas kernels for 0%

profile of v1, /device:TPU:0, one launch (start us, length us, event | category | flops | bytes accessed | tf_op | source)
XLA Modules:
  0.0 147.4 jit_solution(11290325231990856544)
XLA Ops:
  0.6 1.4 collective-permute-start
  4.7 1.5 %convert_element_type.38 = f32[1,2,512,512]{3,2,1,0:T(8,128)S(1)} convert(bf16[1,2,512,512]{3,2,1,0:T(8,128)(2,1)} %param.6) | non-fusion elementwise | flops 524288 | bytes 3145728 | tf_op jit(solution)/shard_map/convert_element_type | solution.py:98
  6.8 1.4 cholesky.16
  11.1 1.3 compare_convert_fusion
  19.6 1.9 %reduce_sum.37 = f32[128,512]{1,0:T(8,128)S(1)} reduce(f32[128,4,512]{2,1,0:T(4,128)} %add.287, f32[]{:T(128)} %constant.136.clone.1), dimensions={1}, to_apply=%region_1.2 | reduce | flops 196608 | bytes 1310724 | tf_op jit(solution)/shard_map/reduce_sum | solution.py:27
  22.0 1.5 %convert_element_type.39 = f32[1,2,512,512]{3,2,1,0:T(8,128)S(1)} convert(bf16[1,2,512,512]{3,2,1,0:T(8,128)(2,1)} %collective-permute-done) | non-fusion elementwise | flops 524288 | bytes 3145728 | tf_op jit(solution)/shard_map/convert_element_type | solution.py:104
  23.6 1.3 copy-done
  26.4 5.4 %collective-permute-done.2 = bf16[1,2,512,512]{3,2,1,0:T(8,128)(2,1)} collective-permute-done((bf16[1,2,512,512]{3,2,1,0:T(8,128)(2,1)}, bf16[1,2,512,512]{3,2,1,0:T(8,128)(2,1)}, u32[]{:S(2)}, u32[]{:S(2)}) %collective-permute-start.2) | collective-permute-done | bytes 1048608 | tf_op jit(solution)/shard_map/ppermute | solution.py:14
  31.8 1.5 %convert_element_type.41 = f32[1,2,512,512]{3,2,1,0:T(8,128)S(1)} convert(bf16[1,2,512,512]{3,2,1,0:T(8,128)(2,1)} %collective-permute-done.2) | non-fusion elementwise | flops 524288 | bytes 3145728 | tf_op jit(solution)/shard_map/convert_element_type | solution.py:104
  34.5 16.1 %collective-permute-done.1 = bf16[1,2,512,512]{3,2,1,0:T(8,128)(2,1)} collective-permute-done((bf16[1,2,512,512]{3,2,1,0:T(8,128)(2,1)}, bf16[1,2,512,512]{3,2,1,0:T(8,128)(2,1)}, u32[]{:S(2)}, u32[]{:S(2)}) %collective-permute-start.1) | collective-permute-done | bytes 1048608 | tf_op jit(solution)/shard_map/ppermute | solution.py:14
  50.6 1.5 %convert_element_type.40 = f32[1,2,512,512]{3,2,1,0:T(8,128)S(1)} convert(bf16[1,2,512,512]{3,2,1,0:T(8,128)(2,1)} %collective-permute-done.1) | non-fusion elementwise | flops 524288 | bytes 3145728 | tf_op jit(solution)/shard_map/convert_element_type | solution.py:104
  52.4 1.3 copy-done.1
  54.0 13.0 %fusion.4 = (f32[512,512]{1,0:T(8,128)}, f32[1,1,512,512]{3,2,1,0:T(8,128)S(1)}, f32[1,1,512,512]{3,2,1,0:T(8,128)S(1)}, f32[512,512]{1,0:T(8,128)}, f32[1,1,512...) fusion(f32[512,512]{1,0:T(8,128)S(1)} %copy-done.10, ...), kind=kLoop, calls=%fused_computation.19 | loop fusion | flops 7864320 | bytes 18874380 | tf_op jit(solution)/shard_map/add | solution.py:42
  67.0 12.5 %fusion.5 = (f32[512,512]{1,0:T(8,128)}, f32[512,512]{1,0:T(8,128)}, f32[512,512]{1,0:T(8,128)}) fusion(f32[1,1,512,512]{3,2,1,0:T(8,128)S(1)} %get-tuple-element.4, f32[1,1,512,512]{3,2,1,0:T(8,128)S(1)} %get-tuple-element.3, f32[512,512]{1,0:T(8,128)S(1)} %copy-done.10, f32[]{:T(128)} %bitcast.1, f32[1,1,512,512]{3,2,1,0:T(8,128)S(1)} %get-tuple-element.16, ...), kind=kLoop, calls=%fused_computation.20 | loop fusion | flops 3145728 | bytes 10485772 | tf_op jit(solution)/shard_map/sub | solution.py:43
  79.5 2.7 %stack.61 = f32[1,128,4,512]{3,2,1,0:T(4,128)} reshape(f32[512,512]{1,0:T(8,128)} %get-tuple-element.17) | data formatting | bytes 2097152 | tf_op jit(solution)/shard_map/stack | solution.py:45
  82.2 1.3 stack.60
  84.8 2.7 %stack.71 = f32[1,128,4,512]{3,2,1,0:T(4,128)} reshape(f32[512,512]{1,0:T(8,128)} %get-tuple-element.19) | data formatting | bytes 2097152 | tf_op jit(solution)/shard_map/stack | solution.py:45
  87.5 1.3 stack.70
  88.8 3.9 %maximum_reduce_fusion = f32[3,128,512]{2,1,0:T(8,128)S(1)} fusion(f32[1,128,4,512]{3,2,1,0:T(4,128)S(1)} %copy-done.6, f32[1,128,4,512]{3,2,1,0:T(4,128)} %stack.61, f32[1,128,4,512]{3,2,1,0:T(4,128)} %stack.60), kind=kLoop, calls=%fused_computation.1 | loop fusion | flops 2162688 | bytes 3932160 | tf_op jit(solution)/shard_map/reduce_sum | solution.py:27
  93.6 2.1 %maximum_reduce_fusion.2 = f32[3,128,512]{2,1,0:T(8,128)S(1)} fusion(f32[1,128,4,512]{3,2,1,0:T(4,128)S(1)} %copy-done.7, f32[1,128,4,512]{3,2,1,0:T(4,128)S(1)} %copy-done.8, f32[1,128,4,512]{3,2,1,0:T(4,128)S(1)} %copy-done.9), kind=kLoop, calls=%fused_computation.3 | loop fusion | flops 2162688 | bytes 3932160 | tf_op jit(solution)/shard_map/reduce_sum | solution.py:27
  96.9 1.5 %stack.66 = f32[1,128,4,512]{3,2,1,0:T(4,128)S(1)} reshape(f32[512,512]{1,0:T(8,128)} %get-tuple-element.18) | data formatting | bytes 2097152 | tf_op jit(solution)/shard_map/stack | solution.py:45
  99.7 3.4 %maximum_reduce_fusion.1 = f32[3,128,512]{2,1,0:T(8,128)S(1)} fusion(f32[1,128,4,512]{3,2,1,0:T(4,128)S(1)} %stack.67, f32[1,128,4,512]{3,2,1,0:T(4,128)S(1)} %stack.66, f32[1,128,4,512]{3,2,1,0:T(4,128)} %stack.65), kind=kLoop, calls=%fused_computation.2 | loop fusion | flops 2162688 | bytes 3932160 | tf_op jit(solution)/shard_map/reduce_sum | solution.py:27
  104.8 3.3 %collective-permute-start.3 = (f32[1,3,8,32]{3,2,1,0:T(8,128)S(1)}, f32[1,3,8,32]{3,2,1,0:T(8,128)S(1)}, u32[]{:S(2)}, u32[]{:S(2)}) collective-permute-start(f32[1,3,8,32]{3,2,1,0:T(8,128)S(1)} %bitcast.211), channel_id=1, source_target_pairs={{0,1},{1,0},{2,3},{3,2},{4,5},{5,4},{6,7},{7,6},{8,9},{9,8},{10,11... | collective-permute-start | bytes 9224 | tf_op jit(solution)/shard_map/ppermute | solution.py:132
  108.1 12.2 %collective-permute-start.4 = (f32[1,3,8,32]{3,2,1,0:T(8,128)S(1)}, f32[1,3,8,32]{3,2,1,0:T(8,128)S(1)}, u32[]{:S(2)}, u32[]{:S(2)}) collective-permute-start(f32[1,3,8,32]{3,2,1,0:T(8,128)S(1)} %bitcast.210), channel_id=1, source_target_pairs={{0,2},{1,3},{2,0},{3,1},{4,6},{5,7},{6,4},{7,5},{8,10},{9,11},{10,... | collective-permute-start | bytes 9224 | tf_op jit(solution)/shard_map/ppermute | solution.py:132
  120.5 1.6 %collective-permute-start.6 = (f32[1,3,8,32]{3,2,1,0:T(8,128)S(1)}, f32[1,3,8,32]{3,2,1,0:T(8,128)S(1)}, u32[]{:S(2)}, u32[]{:S(2)}) collective-permute-start(f32[1,3,8,32]{3,2,1,0:T(8,128)S(1)} %bitcast.207), channel_id=1, source_target_pairs={{0,4},{1,5},{2,6},{3,7},{4,0},{5,1},{6,2},{7,3},{8,12},{9,13},{10,... | collective-permute-start | bytes 9224 | tf_op jit(solution)/shard_map/ppermute | solution.py:132
  123.7 2.8 %collective-permute-start.8 = (f32[1,3,8,32]{3,2,1,0:T(8,128)S(1)}, f32[1,3,8,32]{3,2,1,0:T(8,128)S(1)}, u32[]{:S(2)}, u32[]{:S(2)}) collective-permute-start(f32[1,3,8,32]{3,2,1,0:T(8,128)S(1)} %bitcast.208), channel_id=1, source_target_pairs={{0,6},{1,7},{2,4},{3,5},{4,2},{5,3},{6,0},{7,1},{8,14},{9,15},{10,... | collective-permute-start | bytes 9224 | tf_op jit(solution)/shard_map/ppermute | solution.py:132
  126.7 2.4 %collective-permute-start.10 = (f32[1,3,8,32]{3,2,1,0:T(8,128)S(1)}, f32[1,3,8,32]{3,2,1,0:T(8,128)S(1)}, u32[]{:S(2)}, u32[]{:S(2)}) collective-permute-start(f32[1,3,8,32]{3,2,1,0:T(8,128)S(1)} %bitcast.204), channel_id=1, source_target_pairs={{0,8},{1,9},{2,10},{3,11},{4,12},{5,13},{6,14},{7,15},{8,0},{9,1},... | collective-permute-start | bytes 9224 | tf_op jit(solution)/shard_map/ppermute | solution.py:132
  129.2 3.7 %collective-permute-start.12 = (f32[1,3,8,32]{3,2,1,0:T(8,128)S(1)}, f32[1,3,8,32]{3,2,1,0:T(8,128)S(1)}, u32[]{:S(2)}, u32[]{:S(2)}) collective-permute-start(f32[1,3,8,32]{3,2,1,0:T(8,128)S(1)} %bitcast.202), channel_id=1, source_target_pairs={{0,10},{1,11},{2,8},{3,9},{4,14},{5,15},{6,12},{7,13},{8,2},{9,3},... | collective-permute-start | bytes 9224 | tf_op jit(solution)/shard_map/ppermute | solution.py:132
  133.1 2.4 %collective-permute-start.14 = (f32[1,3,8,32]{3,2,1,0:T(8,128)S(1)}, f32[1,3,8,32]{3,2,1,0:T(8,128)S(1)}, u32[]{:S(2)}, u32[]{:S(2)}) collective-permute-start(f32[1,3,8,32]{3,2,1,0:T(8,128)S(1)} %bitcast.200), channel_id=1, source_target_pairs={{0,12},{1,13},{2,14},{3,15},{4,8},{5,9},{6,10},{7,11},{8,4},{9,5},... | collective-permute-start | bytes 9224 | tf_op jit(solution)/shard_map/ppermute | solution.py:132
  136.4 3.4 %collective-permute-start.16 = (f32[1,3,8,32]{3,2,1,0:T(8,128)S(1)}, f32[1,3,8,32]{3,2,1,0:T(8,128)S(1)}, u32[]{:S(2)}, u32[]{:S(2)}) collective-permute-start(f32[1,3,8,32]{3,2,1,0:T(8,128)S(1)} %bitcast.198), channel_id=1, source_target_pairs={{0,14},{1,15},{2,12},{3,13},{4,10},{5,11},{6,8},{7,9},{8,6},{9,7},... | collective-permute-start | bytes 9224 | tf_op jit(solution)/shard_map/ppermute | solution.py:132
  141.1 1.6 %collective-permute-done.16 = f32[1,3,8,32]{3,2,1,0:T(8,128)S(1)} collective-permute-done((f32[1,3,8,32]{3,2,1,0:T(8,128)S(1)}, f32[1,3,8,32]{3,2,1,0:T(8,128)S(1)}, u32[]{:S(2)}, u32[]{:S(2)}) %collective-permute-start.16) | collective-permute-done | bytes 3104 | tf_op jit(solution)/shard_map/ppermute | solution.py:132
  142.8 2.9 %collective-permute-done.17 = f32[1,3,8,32]{3,2,1,0:T(8,128)S(1)} collective-permute-done((f32[1,3,8,32]{3,2,1,0:T(8,128)S(1)}, f32[1,3,8,32]{3,2,1,0:T(8,128)S(1)}, u32[]{:S(2)}, u32[]{:S(2)}) %collective-permute-start.17) | collective-permute-done | bytes 3104 | tf_op jit(solution)/shard_map/ppermute | solution.py:132
  (121 shorter events, 25.3 us)
Async XLA Ops:
  0.6 5.6 %copy-start.11 = (s32[16,3]{0,1:T(4,128)S(1)}, s32[16,3]{0,1:T(4,128)}, u32[]{:S(2)}) copy-start(s32[16,3]{0,1:T(4,128)} %param.9) | copy-start | bytes 580
  0.6 8.9 %copy-start.13 = (s32[16]{0:T(128)S(1)}, s32[16]{0:T(128)}, u32[]{:S(2)}) copy-start(s32[16]{0:T(128)} %param.11) | copy-start | bytes 196
  0.6 21.4 %collective-permute-start = (bf16[1,2,512,512]{3,2,1,0:T(8,128)(2,1)}, bf16[1,2,512,512]{3,2,1,0:T(8,128)(2,1)}, u32[]{:S(2)}, u32[]{:S(2)}) collective-permute-start(bf16[1,2,512,512]{3,2,1,0:T(8,128)(2,1)} %param.6), channel_id=1, source_target_pairs={{1,0},{2,1},{3,2},{4,3},{5,4},{6,5},{7,6},{8,7},{9,8},{10,9},{11,1... | collective-permute-start | bytes 3145736 | tf_op jit(solution)/shard_map/ppermute | solution.py:14
  2.1 29.7 %collective-permute-start.2 = (bf16[1,2,512,512]{3,2,1,0:T(8,128)(2,1)}, bf16[1,2,512,512]{3,2,1,0:T(8,128)(2,1)}, u32[]{:S(2)}, u32[]{:S(2)}) collective-permute-start(bf16[1,2,512,512]{3,2,1,0:T(8,128)(2,1)} %param.6), channel_id=1, source_target_pairs={{3,0},{4,1},{5,2},{6,3},{7,4},{8,5},{9,6},{10,7},{11,8},{12,9},{13... | collective-permute-start | bytes 3145736 | tf_op jit(solution)/shard_map/ppermute | solution.py:14
  3.4 47.3 %collective-permute-start.1 = (bf16[1,2,512,512]{3,2,1,0:T(8,128)(2,1)}, bf16[1,2,512,512]{3,2,1,0:T(8,128)(2,1)}, u32[]{:S(2)}, u32[]{:S(2)}) collective-permute-start(bf16[1,2,512,512]{3,2,1,0:T(8,128)(2,1)} %param.6), channel_id=1, source_target_pairs={{2,0},{3,1},{4,2},{5,3},{6,4},{7,5},{8,6},{9,7},{10,8},{11,9},{12,... | collective-permute-start | bytes 3145736 | tf_op jit(solution)/shard_map/ppermute | solution.py:14
  6.2 6.6 %copy-start.12 = (f32[16]{0:T(128)S(1)}, f32[16]{0:T(128)}, u32[]{:S(2)}) copy-start(f32[16]{0:T(128)} %param.8) | copy-start | bytes 196
  23.6 1.3 copy-start
  52.2 1.6 %copy-start.1 = (f32[1,2,512,512]{3,2,1,0:T(8,128)S(1)}, f32[1,2,512,512]{3,2,1,0:T(8,128)}, u32[]{:S(2)}) copy-start(f32[1,2,512,512]{3,2,1,0:T(8,128)} %copy-done) | copy-start | bytes 6291460
  52.2 1.9 %copy-start.10 = (f32[512,512]{1,0:T(8,128)S(1)}, f32[512,512]{1,0:T(8,128)}, u32[]{:S(2)}) copy-start(f32[512,512]{1,0:T(8,128)} %param.7) | copy-start | bytes 3145732
  79.5 2.7 %copy-start.5 = (f32[512,512]{1,0:T(8,128)S(1)}, f32[512,512]{1,0:T(8,128)}, u32[]{:S(2)}) copy-start(f32[512,512]{1,0:T(8,128)} %get-tuple-element.2) | copy-start | bytes 3145732
  79.5 4.0 %copy-start.3 = (f32[1,1,512,512]{3,2,1,0:T(8,128)S(1)}, f32[1,1,512,512]{3,2,1,0:T(8,128)}, u32[]{:S(2)}) copy-start(f32[1,1,512,512]{3,2,1,0:T(8,128)} %multiply_add_fusion) | copy-start | bytes 3145732
  83.5 3.9 %copy-start.4 = (f32[512,512]{1,0:T(8,128)S(1)}, f32[512,512]{1,0:T(8,128)}, u32[]{:S(2)}) copy-start(f32[512,512]{1,0:T(8,128)} %get-tuple-element.11) | copy-start | bytes 3145732
  84.8 4.0 %copy-start.6 = (f32[1,128,4,512]{3,2,1,0:T(4,128)S(1)}, f32[1,128,4,512]{3,2,1,0:T(4,128)}, u32[]{:S(2)}) copy-start(f32[1,128,4,512]{3,2,1,0:T(4,128)} %stack.62) | copy-start | bytes 3145732
  88.8 4.8 %copy-start.7 = (f32[1,128,4,512]{3,2,1,0:T(4,128)S(1)}, f32[1,128,4,512]{3,2,1,0:T(4,128)}, u32[]{:S(2)}) copy-start(f32[1,128,4,512]{3,2,1,0:T(4,128)} %stack.72) | copy-start | bytes 3145732
  88.8 4.8 %copy-start.8 = (f32[1,128,4,512]{3,2,1,0:T(4,128)S(1)}, f32[1,128,4,512]{3,2,1,0:T(4,128)}, u32[]{:S(2)}) copy-start(f32[1,128,4,512]{3,2,1,0:T(4,128)} %stack.71) | copy-start | bytes 3145732
  88.8 4.8 %copy-start.9 = (f32[1,128,4,512]{3,2,1,0:T(4,128)S(1)}, f32[1,128,4,512]{3,2,1,0:T(4,128)}, u32[]{:S(2)}) copy-start(f32[1,128,4,512]{3,2,1,0:T(4,128)} %stack.70) | copy-start | bytes 3145732
  96.6 1.9 %copy-start.2 = (f32[512,512]{1,0:T(8,128)S(1)}, f32[512,512]{1,0:T(8,128)}, u32[]{:S(2)}) copy-start(f32[512,512]{1,0:T(8,128)} %get-tuple-element.14) | copy-start | bytes 3145732
  104.8 19.0 %collective-permute-start.3 = (f32[1,3,8,32]{3,2,1,0:T(8,128)S(1)}, f32[1,3,8,32]{3,2,1,0:T(8,128)S(1)}, u32[]{:S(2)}, u32[]{:S(2)}) collective-permute-start(f32[1,3,8,32]{3,2,1,0:T(8,128)S(1)} %bitcast.211), channel_id=1, source_target_pairs={{0,1},{1,0},{2,3},{3,2},{4,5},{5,4},{6,7},{7,6},{8,9},{9,8},{10,11... | collective-permute-start | bytes 9224 | tf_op jit(solution)/shard_map/ppermute | solution.py:132
  108.1 18.4 %collective-permute-start.4 = (f32[1,3,8,32]{3,2,1,0:T(8,128)S(1)}, f32[1,3,8,32]{3,2,1,0:T(8,128)S(1)}, u32[]{:S(2)}, u32[]{:S(2)}) collective-permute-start(f32[1,3,8,32]{3,2,1,0:T(8,128)S(1)} %bitcast.210), channel_id=1, source_target_pairs={{0,2},{1,3},{2,0},{3,1},{4,6},{5,7},{6,4},{7,5},{8,10},{9,11},{10,... | collective-permute-start | bytes 9224 | tf_op jit(solution)/shard_map/ppermute | solution.py:132
  120.3 6.4 %collective-permute-start.5 = (f32[1,3,8,32]{3,2,1,0:T(8,128)S(1)}, f32[1,3,8,32]{3,2,1,0:T(8,128)S(1)}, u32[]{:S(2)}, u32[]{:S(2)}) collective-permute-start(f32[1,3,8,32]{3,2,1,0:T(8,128)S(1)} %bitcast.209), channel_id=1, source_target_pairs={{0,3},{1,2},{2,1},{3,0},{4,7},{5,6},{6,5},{7,4},{8,11},{9,10},{10,... | collective-permute-start | bytes 9224 | tf_op jit(solution)/shard_map/ppermute | solution.py:132
  120.5 8.6 %collective-permute-start.6 = (f32[1,3,8,32]{3,2,1,0:T(8,128)S(1)}, f32[1,3,8,32]{3,2,1,0:T(8,128)S(1)}, u32[]{:S(2)}, u32[]{:S(2)}) collective-permute-start(f32[1,3,8,32]{3,2,1,0:T(8,128)S(1)} %bitcast.207), channel_id=1, source_target_pairs={{0,4},{1,5},{2,6},{3,7},{4,0},{5,1},{6,2},{7,3},{8,12},{9,13},{10,... | collective-permute-start | bytes 9224 | tf_op jit(solution)/shard_map/ppermute | solution.py:132
  122.2 7.0 %collective-permute-start.7 = (f32[1,3,8,32]{3,2,1,0:T(8,128)S(1)}, f32[1,3,8,32]{3,2,1,0:T(8,128)S(1)}, u32[]{:S(2)}, u32[]{:S(2)}) collective-permute-start(f32[1,3,8,32]{3,2,1,0:T(8,128)S(1)} %bitcast.206), channel_id=1, source_target_pairs={{0,5},{1,4},{2,7},{3,6},{4,1},{5,0},{6,3},{7,2},{8,13},{9,12},{10,... | collective-permute-start | bytes 9224 | tf_op jit(solution)/shard_map/ppermute | solution.py:132
  123.7 9.1 %collective-permute-start.8 = (f32[1,3,8,32]{3,2,1,0:T(8,128)S(1)}, f32[1,3,8,32]{3,2,1,0:T(8,128)S(1)}, u32[]{:S(2)}, u32[]{:S(2)}) collective-permute-start(f32[1,3,8,32]{3,2,1,0:T(8,128)S(1)} %bitcast.208), channel_id=1, source_target_pairs={{0,6},{1,7},{2,4},{3,5},{4,2},{5,3},{6,0},{7,1},{8,14},{9,15},{10,... | collective-permute-start | bytes 9224 | tf_op jit(solution)/shard_map/ppermute | solution.py:132
  126.5 6.5 %collective-permute-start.9 = (f32[1,3,8,32]{3,2,1,0:T(8,128)S(1)}, f32[1,3,8,32]{3,2,1,0:T(8,128)S(1)}, u32[]{:S(2)}, u32[]{:S(2)}) collective-permute-start(f32[1,3,8,32]{3,2,1,0:T(8,128)S(1)} %bitcast.205), channel_id=1, source_target_pairs={{0,7},{1,6},{2,5},{3,4},{4,3},{5,2},{6,1},{7,0},{8,15},{9,14},{10,... | collective-permute-start | bytes 9224 | tf_op jit(solution)/shard_map/ppermute | solution.py:132
  126.7 8.7 %collective-permute-start.10 = (f32[1,3,8,32]{3,2,1,0:T(8,128)S(1)}, f32[1,3,8,32]{3,2,1,0:T(8,128)S(1)}, u32[]{:S(2)}, u32[]{:S(2)}) collective-permute-start(f32[1,3,8,32]{3,2,1,0:T(8,128)S(1)} %bitcast.204), channel_id=1, source_target_pairs={{0,8},{1,9},{2,10},{3,11},{4,12},{5,13},{6,14},{7,15},{8,0},{9,1},... | collective-permute-start | bytes 9224 | tf_op jit(solution)/shard_map/ppermute | solution.py:132
  129.2 7.2 %collective-permute-start.11 = (f32[1,3,8,32]{3,2,1,0:T(8,128)S(1)}, f32[1,3,8,32]{3,2,1,0:T(8,128)S(1)}, u32[]{:S(2)}, u32[]{:S(2)}) collective-permute-start(f32[1,3,8,32]{3,2,1,0:T(8,128)S(1)} %bitcast.203), channel_id=1, source_target_pairs={{0,9},{1,8},{2,11},{3,10},{4,13},{5,12},{6,15},{7,14},{8,1},{9,0},... | collective-permute-start | bytes 9224 | tf_op jit(solution)/shard_map/ppermute | solution.py:132
  129.2 10.6 %collective-permute-start.12 = (f32[1,3,8,32]{3,2,1,0:T(8,128)S(1)}, f32[1,3,8,32]{3,2,1,0:T(8,128)S(1)}, u32[]{:S(2)}, u32[]{:S(2)}) collective-permute-start(f32[1,3,8,32]{3,2,1,0:T(8,128)S(1)} %bitcast.202), channel_id=1, source_target_pairs={{0,10},{1,11},{2,8},{3,9},{4,14},{5,15},{6,12},{7,13},{8,2},{9,3},... | collective-permute-start | bytes 9224 | tf_op jit(solution)/shard_map/ppermute | solution.py:132
  132.9 8.2 %collective-permute-start.13 = (f32[1,3,8,32]{3,2,1,0:T(8,128)S(1)}, f32[1,3,8,32]{3,2,1,0:T(8,128)S(1)}, u32[]{:S(2)}, u32[]{:S(2)}) collective-permute-start(f32[1,3,8,32]{3,2,1,0:T(8,128)S(1)} %bitcast.201), channel_id=1, source_target_pairs={{0,11},{1,10},{2,9},{3,8},{4,15},{5,14},{6,13},{7,12},{8,3},{9,2},... | collective-permute-start | bytes 9224 | tf_op jit(solution)/shard_map/ppermute | solution.py:132
  133.1 8.0 %collective-permute-start.14 = (f32[1,3,8,32]{3,2,1,0:T(8,128)S(1)}, f32[1,3,8,32]{3,2,1,0:T(8,128)S(1)}, u32[]{:S(2)}, u32[]{:S(2)}) collective-permute-start(f32[1,3,8,32]{3,2,1,0:T(8,128)S(1)} %bitcast.200), channel_id=1, source_target_pairs={{0,12},{1,13},{2,14},{3,15},{4,8},{5,9},{6,10},{7,11},{8,4},{9,5},... | collective-permute-start | bytes 9224 | tf_op jit(solution)/shard_map/ppermute | solution.py:132
  135.5 5.6 %collective-permute-start.15 = (f32[1,3,8,32]{3,2,1,0:T(8,128)S(1)}, f32[1,3,8,32]{3,2,1,0:T(8,128)S(1)}, u32[]{:S(2)}, u32[]{:S(2)}) collective-permute-start(f32[1,3,8,32]{3,2,1,0:T(8,128)S(1)} %bitcast.199), channel_id=1, source_target_pairs={{0,13},{1,12},{2,15},{3,14},{4,9},{5,8},{6,11},{7,10},{8,5},{9,4},... | collective-permute-start | bytes 9224 | tf_op jit(solution)/shard_map/ppermute | solution.py:132
  136.4 6.4 %collective-permute-start.16 = (f32[1,3,8,32]{3,2,1,0:T(8,128)S(1)}, f32[1,3,8,32]{3,2,1,0:T(8,128)S(1)}, u32[]{:S(2)}, u32[]{:S(2)}) collective-permute-start(f32[1,3,8,32]{3,2,1,0:T(8,128)S(1)} %bitcast.198), channel_id=1, source_target_pairs={{0,14},{1,15},{2,12},{3,13},{4,10},{5,11},{6,8},{7,9},{8,6},{9,7},... | collective-permute-start | bytes 9224 | tf_op jit(solution)/shard_map/ppermute | solution.py:132
  139.8 5.9 %collective-permute-start.17 = (f32[1,3,8,32]{3,2,1,0:T(8,128)S(1)}, f32[1,3,8,32]{3,2,1,0:T(8,128)S(1)}, u32[]{:S(2)}, u32[]{:S(2)}) collective-permute-start(f32[1,3,8,32]{3,2,1,0:T(8,128)S(1)} %bitcast.197), channel_id=1, source_target_pairs={{0,15},{1,14},{2,13},{3,12},{4,11},{5,10},{6,9},{7,8},{8,7},{9,6},... | collective-permute-start | bytes 9224 | tf_op jit(solution)/shard_map/ppermute | solution.py:132
